TPU v7x, 32 devices: a whole 2x2x4 slice. The times are simulated.
32 devices in a mesh: dp: 4 (over z), cent: 8 (over y, x, core).
Axes of the slice: x: 2, y: 2, z: 4, core: 2. Of those that a mesh axis runs over, the one named last changes fastest.
Arguments:
- points: bfloat16 [4096, 1024], P(('dp', 'cent')), may hold values from -6 to 6
- centroids: bfloat16 [32768, 1024], P('cent'), may hold values from -6 to 6
Outputs:
- centroids_next: float32 [1024, 32768], P('dp', 'cent')
All inputs are finite; a program needn't handle non-finite values.
Results may differ from a plain program's by a relative error of at most 0.007.
Values may be sent and summed in bfloat16 or wider, within the bound.
A program may use at most 128 MiB of HBM per device.

v0:
```python
import jax
import jax.numpy as jnp
from jax import lax
from jax.sharding import PartitionSpec as P

BETA_GAIN = 4.0
PRIOR = 0.5


def local(points, centroids):
    features = points.shape[1]
    sharpness = BETA_GAIN * features ** (-0.5)
    gathered = lax.all_gather(points, "cent", axis=0, tiled=True)
    sqnorm = jnp.sum(jnp.square(centroids.astype(jnp.float32)), axis=1)
    total_rows = gathered.shape[0]
    block_rows = min(512, total_rows)
    blocks = gathered.reshape(total_rows // block_rows, block_rows, features)
    shard_cents = centroids.shape[0]

    def logits_of(xblock):
        dots = lax.dot_general(
            xblock, centroids, (((1,), (1,)), ((), ())), preferred_element_type=jnp.float32
        )
        return sharpness * (dots - 0.5 * sqnorm[None, :])

    def resp_of(logits, row_top, row_total):
        return (jnp.exp(logits - row_top[:, None]) / row_total[:, None]).astype(jnp.bfloat16)

    logits = lax.map(logits_of, blocks)
    local_max = jnp.max(logits, axis=-1)
    local_sum = jnp.sum(jnp.exp(logits - local_max[..., None]), axis=-1)
    row_top = lax.pmax(local_max, "cent")
    row_total = lax.psum(local_sum * jnp.exp(local_max - row_top), "cent")
    resp = jax.vmap(resp_of)(logits, row_top, row_total)
    resp = resp.reshape(total_rows, shard_cents)
    counts = jnp.sum(resp.astype(jnp.float32), axis=0)
    dp_count = lax.axis_size("dp")
    dp_index = lax.axis_index("dp")
    column_share = features // dp_count
    numer = lax.psum_scatter(
        lax.dot_general(
            gathered, resp, (((0,), (0,)), ((), ())), preferred_element_type=jnp.float32
        ).astype(jnp.bfloat16),
        "dp",
        scatter_dimension=0,
        tiled=True,
    ).astype(jnp.float32)
    counts_all = lax.psum(counts, "dp")
    own_cols = (
        lax.dynamic_slice_in_dim(centroids, dp_index * column_share, column_share, 1)
        .astype(jnp.float32)
        .T
    )
    result = (numer + PRIOR * own_cols) / (counts_all[None, :] + PRIOR)
    return result


def solution(mesh):
    return jax.shard_map(
        local,
        mesh=mesh,
        in_specs=(P(("dp", "cent"), None), P("cent", None)),
        out_specs=P("dp", "cent"),
        check_vma=False,
    )
```

profile of v0, /device:TPU:0, one launch (start us, length us, event | category | flops | bytes accessed | tf_op | source)
XLA Modules:
  0.0 283.1 jit_solution(1797543977805885158)
XLA Ops:
  6.5 0.0 all-gather.2.cloned.1.call-start
  6.5 0.7 all-gather.2.cloned.1.call-update
  7.3 0.0 reduce-scatter.2.cloned.1.call-start
  7.3 5.1 %multiply_reduce_fusion = f32[4096]{0:T(1024)S(1)} fusion(bf16[4096,1024]{1,0:T(8,128)(2,1)} %param.5), kind=kLoop, calls=%fused_computation.8 | loop fusion | flops 12578816 | bytes 8404992 | tf_op jit(solution)/shard_map/reduce_sum | solution.py:14
  12.4 27.5 %all-gather.2.cloned.1.call-done = bf16[1024,1024]{1,0:T(8,128)(2,1)} async-done(((bf16[128,1024]{1,0:T(8,128)(2,1)}), bf16[1024,1024]{1,0:T(8,128)(2,1)}) %all-gather.2.cloned.1.call-update) | async-done | bytes 2097168 | tf_op jit(solution)/shard_map/all_gather | solution.py:13
  39.9 23.0 %while.10 = (s32[]{:T(128)}, f32[2,512,4096]{2,1,0:T(8,128)}, bf16[2,512,1024]{2,1,0:T(8,128)(2,1)}, bf16[4096,1024]{1,0:T(8,128)(2,1)}, f32[4096]{0:T(1024)S(1)}, /*index=5*/s32[]{:T(128)}) while((s32[]{:T(128)}, f32[2,512,4096]{2,1,0:T(8,128)}, bf16[2,512,1024]{2,1,0:T(8,128)(2,1)}, bf16[4096,1024]{1,0:T(8,128)(2,1)}, f32[4096]{0:T(1024)S(1)}, ...), condition=%wide.region_2.3_spmd, body=%wide.region_1.2_spmd.sunk | while | flops 4299165696 | bytes 17876036 | solution.py:29
  39.9 11.5 %bitcast_dynamic-update-slice_fusion.2 = f32[2,512,4096]{2,1,0:T(8,128)} fusion(f32[2,512,4096]{2,1,0:T(8,128)} %get-tuple-element.83, s32[]{:T(128)} %get-tuple-element.82, bf16[4096,1024]{1,0:T(8,128)(2,1)} %get-tuple-element.91, f32[4096]{0:T(1024)S(1)} %broadcast_multiply_fusion.2, bf16[2,512,1024]{2,1,0:T(8,128)(2,1)} %get-tuple-element.90), kind=kOutput, calls=%fused_computation.clone.1 | convolution fusion | flops 4299161600 | bytes 17843200 | tf_op jit(solution)/shard_map/while/body/eval_jaxpr/dot_general | solution.py:21
  51.4 11.5 %bitcast_dynamic-update-slice_fusion.2 = f32[2,512,4096]{2,1,0:T(8,128)} fusion(f32[2,512,4096]{2,1,0:T(8,128)} %get-tuple-element.83, s32[]{:T(128)} %get-tuple-element.82, bf16[4096,1024]{1,0:T(8,128)(2,1)} %get-tuple-element.91, f32[4096]{0:T(1024)S(1)} %broadcast_multiply_fusion.2, bf16[2,512,1024]{2,1,0:T(8,128)(2,1)} %get-tuple-element.90), kind=kOutput, calls=%fused_computation.clone.1 | convolution fusion | flops 4299161600 | bytes 17843200 | tf_op jit(solution)/shard_map/while/body/eval_jaxpr/dot_general | solution.py:21
  62.8 6.6 %reduce_max.9 = f32[2,512]{1,0:T(2,128)S(1)} reduce(f32[2,512,4096]{2,1,0:T(8,128)} %get-tuple-element.32, f32[]{:T(128)} %constant.10.clone.1), dimensions={2}, to_apply=%region_3.4 | reduce | flops 4193280 | bytes 16781316 | tf_op jit(solution)/shard_map/reduce_max | solution.py:30
  69.4 8.1 %exponential_reduce_fusion = f32[2,512]{1,0:T(2,128)S(1)} fusion(f32[2,512,4096]{2,1,0:T(8,128)} %get-tuple-element.32, f32[2,512]{1,0:T(2,128)S(1)} %reduce_max.9), kind=kLoop, calls=%fused_computation.7 | loop fusion | flops 8387584 | bytes 16785408 | tf_op jit(solution)/shard_map/reduce_sum | solution.py:31
  77.5 13.1 %pmax.7 = f32[2,512]{1,0:T(2,128)S(1)} all-reduce(f32[2,512]{1,0:T(2,128)S(1)} %reduce_max.9), channel_id=1, replica_groups=mesh['dp'=4,'cent'=8] {'cent'}, use_global_device_ids=true, to_apply=%region_4.5 | all-reduce | flops 1024 | bytes 8192 | tf_op jit(solution)/shard_map/pmax | solution.py:32
  90.6 12.0 %psum.14 = f32[2,512]{1,0:T(2,128)S(1)} all-reduce(f32[2,512]{1,0:T(2,128)S(1)} %exponential_multiply_fusion), channel_id=1, replica_groups=mesh['dp'=4,'cent'=8] {'cent'}, use_global_device_ids=true, to_apply=%region_6.7 | all-reduce | flops 1024 | bytes 8192 | tf_op jit(solution)/shard_map/psum | solution.py:33
  102.6 0.0 copy-start
  102.6 7.9 %convert_reduce_fusion = (f32[4096]{0:T(1024)S(1)}, bf16[2,512,4096]{2,1,0:T(8,128)(2,1)S(1)}) fusion(f32[2,512]{1,0:T(2,128)S(1)} %psum.14, f32[2,512,4096]{2,1,0:T(8,128)} %get-tuple-element.32, f32[2,512]{1,0:T(2,128)S(1)} %pmax.7), kind=kLoop, calls=%fused_computation.5 | loop fusion | flops 20967424 | bytes 25190400 | tf_op jit(solution)/shard_map/reduce_sum | solution.py:36
  110.6 0.0 copy-done
  110.6 11.3 %convert_bitcast_fusion = bf16[1024,4096]{0,1:T(8,128)(2,1)} fusion(bf16[1024,4096]{1,0:T(8,128)(2,1)S(1)} %bitcast.22, bf16[1024,1024]{1,0:T(8,128)(2,1)S(1)} %bitcast.24), kind=kOutput, calls=%fused_computation.9 | convolution fusion | flops 8594128896 | bytes 18874368 | tf_op jit(solution)/shard_map/dot_general | solution.py:41
  121.9 0.0 reduce-scatter.2.cloned.1.call-update
  121.9 19.0 %psum.15 = f32[4096]{0:T(1024)S(1)} all-reduce(f32[4096]{0:T(1024)S(1)} %get-tuple-element.43), channel_id=1, replica_groups=mesh['dp'=4,'cent'=8] {'dp'}, use_global_device_ids=true, to_apply=%region_9.10 | all-reduce | flops 4096 | bytes 32768 | tf_op jit(solution)/shard_map/psum | solution.py:48
  141.0 125.8 %reduce-scatter.2.cloned.1.call-done = bf16[256,4096]{0,1:T(8,128)(2,1)} async-done(((bf16[1024,4096]{0,1:T(8,128)(2,1)}), bf16[256,4096]{0,1:T(8,128)(2,1)}) %reduce-scatter.2.cloned.1.call-update) | async-done | bytes 2097168 | tf_op jit(solution)/shard_map/reduce_scatter | solution.py:40
  266.8 3.9 %fusion.3 = f32[256,4096]{0,1:T(8,128)} fusion(bf16[256,4096]{0,1:T(8,128)(2,1)} %reduce-scatter.2.cloned.1.call-done, f32[4096]{0:T(1024)S(1)} %broadcast_add_fusion, bf16[4096,1024]{1,0:T(8,128)(2,1)} %get-tuple-element.96, s32[]{:T(128)S(6)} %select_n.3), kind=kLoop, calls=%fused_computation.11 | loop fusion | flops 5242880 | bytes 8404996 | tf_op jit(solution)/shard_map/div | solution.py:54
  270.7 5.6 %copy.3 = f32[256,4096]{1,0:T(8,128)} copy(f32[256,4096]{0,1:T(8,128)} %fusion.3) | data formatting | bytes 8388608 | tf_op jit(solution)/shard_map/div | solution.py:54
  (5 shorter events, 0.0 us)
Async XLA Ops:
  6.5 33.3 %all-gather.2.cloned.1.call-start = ((), (), s32[]{:S(2)}) async-start(), calls=%async_computation.1 | async-start | bytes 2359296 | tf_op jit(solution)/shard_map/all_gather | solution.py:13
  7.3 259.5 %reduce-scatter.2.cloned.1.call-start = ((), (), s32[]{:S(2)}) async-start(), calls=%async_computation.2 | async-start | bytes 10485760 | tf_op jit(solution)/shard_map/reduce_scatter | solution.py:40
  102.6 8.0 %copy-start = (bf16[2,512,1024]{2,1,0:T(8,128)(2,1)S(1)}, bf16[2,512,1024]{2,1,0:T(8,128)(2,1)}, u32[]{:S(2)}) copy-start(bf16[2,512,1024]{2,1,0:T(8,128)(2,1)} %get-tuple-element.103) | copy-start | bytes 6291460
Sparse Core Ops, SparseCore 0:
  9.2 30.5 all-gather.1
  122.0 144.7 reduce-scatter.1
where the time goes:
time: 284 us; the launch traced here: 283 us
  waiting for transfers between devices  154 us (54%)
  blocking collectives  44.1 us (16%)
  matrix products  34.2 us (12%)
  other arithmetic  31.6 us (11%)
  between operations  13.5 us (5%)
  local copies, waits for them, and re-layouts  5.6 us (2%)
    reduce_scatter x1, waiting for transfers between devices, local(): lax.psum_scatter(lax.dot_general(gathered, resp, (((0,), (0,)), ((), ()))...  126 us
    all_gather x1, waiting for transfers between devices, local(): gathered = lax.all_gather(points, 'cent', axis=0, tiled=True)  27.5 us
    dot_general x2, matrix products, logits_of(): lax.dot_general(xblock, centroids, (((1,), (1,)), ((), ())), preferred_el...  22.9 us
    psum x1, blocking collectives, local(): counts_all = lax.psum(counts, 'dp')  19 us
    pmax x1, blocking collectives, local(): row_top = lax.pmax(local_max, 'cent')  13.1 us
    psum x1, blocking collectives, local(): row_total = lax.psum(local_sum * jnp.exp(local_max - row_top), 'cent')  12 us
    dot_general x1, matrix products, local(): lax.dot_general(gathered, resp, (((0,), (0,)), ((), ())), preferred_eleme...  11.3 us
    reduce_sum x1, other arithmetic, local(): local_sum = jnp.sum(jnp.exp(logits - local_max[..., None]), axis=-1)  8.1 us
  transfers between devices with their start and end apart: 2, of which 2 were waited for; matrix products, arithmetic and copies ran while one was open for 2% of the time, Pallas kernels for 0%

commit v1 on v0

--- a/solution.py
+++ b/solution.py
@@ -1,13 +1,20 @@
+import functools
+import math
+
 import jax
 import jax.numpy as jnp
 from jax import lax
+from jax.experimental import pallas as pl
+from jax.experimental.pallas import tpu as pltpu
 from jax.sharding import PartitionSpec as P
 
 BETA_GAIN = 4.0
 PRIOR = 0.5
-
-
-def local(points, centroids):
+MESH = pl.DeviceIdType.MESH
+NT = (((1,), (1,)), ((), ()))
+
+
+def general(points, centroids):
     features = points.shape[1]
     sharpness = BETA_GAIN * features ** (-0.5)
     gathered = lax.all_gather(points, "cent", axis=0, tiled=True)
@@ -18,9 +25,7 @@
     shard_cents = centroids.shape[0]
 
     def logits_of(xblock):
-        dots = lax.dot_general(
-            xblock, centroids, (((1,), (1,)), ((), ())), preferred_element_type=jnp.float32
-        )
+        dots = lax.dot_general(xblock, centroids, NT, preferred_element_type=jnp.float32)
         return sharpness * (dots - 0.5 * sqnorm[None, :])
 
     def resp_of(logits, row_top, row_total):
@@ -51,11 +56,325 @@
         .astype(jnp.float32)
         .T
     )
-    result = (numer + PRIOR * own_cols) / (counts_all[None, :] + PRIOR)
-    return result
+    return (numer + PRIOR * own_cols) / (counts_all[None, :] + PRIOR)
+
+
+NZ = 4
+NC = 8
+CHUNK = 1024
+
+
+def fused(
+    points_ref, cents_ref, out_ref,
+    x_ref, c_ref, e_ref, xt_ref, a_ref, bias_ref, buf0, buf1, obuf, mstat, scale_ref, gath,
+    load_sem, send_sem, recv_sem, stat_send, stat_recv, out_sem,
+):
+    shard, feats = points_ref.shape
+    kc = cents_ref.shape[0]
+    n_chunk = kc // CHUNK
+    block = 2 * shard
+    group = NC * shard
+    own_feats = feats // NZ
+    gain = BETA_GAIN * feats ** (-0.5) * math.log2(math.e)
+
+    z = lax.axis_index("dp")
+    cent = lax.axis_index("cent")
+    core = cent % 2
+    xx = (cent // 2) % 2
+    yy = cent // 4
+    flip = z // 2
+    zz = z + flip * (3 - 2 * z)
+
+    def z_of(j):
+        s = (1 - zz) if j == 1 else (zz if j == 0 else j)
+        return s + flip * (3 - 2 * s)
+
+    def pos_of(pos):
+        fx = pos in ("x", "d")
+        fy = pos in ("y", "d")
+        return ((1 - yy) if fy else yy) * 2 + ((1 - xx) if fx else xx)
+
+    x_peer = (z, (yy * 2 + 1 - xx) * 2 + core)
+    y_peer = (z, ((1 - yy) * 2 + xx) * 2 + core)
+    sib = (z, cent + 1 - 2 * core)
+
+    def piece(sid):
+        return x_ref.at[pl.ds(pl.multiple_of(sid * shard, shard), shard)]
+
+    def sid_of(j, pos, other=False):
+        return z_of(j) * NC + pos_of(pos) * 2 + ((1 - core) if other else core)
+
+    def copy_to(sid, dev, slot):
+        return pltpu.make_async_remote_copy(
+            src_ref=piece(sid), dst_ref=piece(sid), send_sem=send_sem.at[slot],
+            recv_sem=recv_sem.at[sid], device_id=dev, device_id_type=MESH,
+        )
+
+    def wait_piece(sid):
+        copy_to(sid, sib, 0).wait_recv()
+
+    POS = {"c": 0, "x": 1, "y": 2, "d": 3}
+
+    def routes(j, pos):
+        base = (j * 4 + POS[pos]) * 5
+        r = []
+        if pos == "c":
+            zj = z_of(j)
+            up = (zj <= z) & (z < NZ - 1)
+            down = (zj >= z) & (z > 0)
+            r.append((up, (z + 1, cent), base))
+            r.append((down, (z - 1, cent), base + 1))
+            r.append((None, x_peer, base + 2))
+            r.append((None, y_peer, base + 3))
+        if pos == "x" and j % 2 == 0:
+            r.append((None, y_peer, base + 3))
+        if pos == "y" and j % 2 == 1:
+            r.append((None, x_peer, base + 2))
+        r.append((None, sib, base + 4))
+        return r
+
+    def each_route(j, pos, act):
+        sid = sid_of(j, pos)
+        for cond, dev, slot in routes(j, pos):
+            if cond is None:
+                act(copy_to(sid, dev, slot))
+            else:
+                @pl.when(cond)
+                def _(dev=dev, slot=slot):
+                    act(copy_to(sid, dev, slot))
+
+    def pass_on(j, pos):
+        if (j, pos) != (0, "c"):
+            wait_piece(sid_of(j, pos))
+        each_route(j, pos, lambda c: c.start())
+
+    own_id = sid_of(0, "c")
+    load_x = pltpu.make_async_copy(points_ref, piece(own_id), load_sem.at[0])
+    load_c = pltpu.make_async_copy(cents_ref, c_ref, load_sem.at[1])
+    load_x.start()
+    load_c.start()
+    barrier = pltpu.get_barrier_semaphore()
+    for d in range(1, NC):
+        pl.semaphore_signal(barrier, inc=1, device_id=(z, (cent + d) % NC), device_id_type=MESH)
+
+    @pl.when(z > 0)
+    def _():
+        pl.semaphore_signal(barrier, inc=1, device_id=(z - 1, cent), device_id_type=MESH)
+
+    @pl.when(z < NZ - 1)
+    def _():
+        pl.semaphore_signal(barrier, inc=1, device_id=(z + 1, cent), device_id_type=MESH)
+
+    inner_z = jnp.minimum(z, 1) * jnp.minimum(NZ - 1 - z, 1)
+    pl.semaphore_wait(barrier, NC + inner_z)
+
+    load_x.wait()
+    pass_on(0, "c")
+    load_c.wait()
+
+    def norm_step(r, _):
+        rows = pl.ds(pl.multiple_of(r * 256, 256), 256)
+        v = c_ref[rows, :].astype(jnp.float32)
+        s = jnp.sum(v * v, axis=1, keepdims=True) * (0.5 * gain)
+        bias_ref[rows, :] = jnp.broadcast_to(s, (256, 128))
+        return 0
+
+    lax.fori_loop(0, kc // 256, norm_step, 0)
+
+    def stat_copy(j, d):
+        zj = z_of(j)
+        return pltpu.make_async_remote_copy(
+            src_ref=gath.at[cent, zj], dst_ref=gath.at[cent, zj],
+            send_sem=stat_send.at[j, d], recv_sem=stat_recv.at[cent, zj],
+            device_id=(z, (cent + d) % NC), device_id_type=MESH,
+        )
+
+    own_col = pl.ds(pl.multiple_of(z * own_feats, own_feats), own_feats)
+    bufs = (buf0, buf1)
+
+    def step(n, _):
+        for at, items in (
+            (1, ((0, "x"), (0, "y"), (1, "c"))),
+            (4, ((0, "d"), (1, "x"), (1, "y"), (2, "c"))),
+            (8, ((1, "d"), (2, "x"), (2, "y"), (3, "c"))),
+            (12, ((2, "d"), (3, "x"), (3, "y"))),
+            (15, ((3, "d"),)),
+        ):
+            @pl.when(n == at)
+            def _(items=items):
+                for j, pos in items:
+                    pass_on(j, pos)
+
+        g, r = n // 4, n % 4
+        last = n // 15
+        first = 1 - jnp.minimum(n, 1)
+        r0 = 1 - jnp.minimum(r, 1)
+        r3 = r // 3
+        j = g - r0 + first + r3 - last
+        fx = jnp.where(r == 1, 1, 0) + r0 - first + last
+        fy = jnp.where(r == 2, 1, 0) + r0 - first + last
+        j1 = jnp.where(j == 1, 1, 0)
+        j0 = jnp.where(j == 0, 1, 0)
+        s = j0 * zz + j1 * (1 - zz) + (1 - j0 - j1) * j
+        zj = s + flip * (3 - 2 * s)
+        py = yy + fy * (1 - 2 * yy)
+        px = xx + fx * (1 - 2 * xx)
+        pid = py * 2 + px
+        wait_piece(zj * NC + pid * 2 + 1 - core)
+        row = pl.multiple_of(zj * group + pid * block, block)
+        rows = pl.ds(row, block)
+        xb = x_ref[rows, :]
+        xt_ref[:, rows] = x_ref[rows, own_col].astype(jnp.float32).T.astype(jnp.bfloat16)
+
+        def dots(c):
+            bufs[c % 2][...] = lax.dot_general(
+                c_ref[c * CHUNK:(c + 1) * CHUNK, :], xb, NT, preferred_element_type=jnp.float32
+            )
+
+        tops, sums = [], []
+
+        def soft(c):
+            ks = slice(c * CHUNK, (c + 1) * CHUNK)
+            b = bias_ref[ks, :]
+            ms, ls = [], []
+            for h in range(block // 128):
+                t = bufs[c % 2][:, h * 128:(h + 1) * 128] * gain - b
+                m = jnp.max(t, axis=0, keepdims=True)
+                e = jnp.exp2(t - m)
+                ls.append(jnp.sum(e, axis=0, keepdims=True))
+                ms.append(m)
+                e_ref[ks, pl.ds(pl.multiple_of(row + h * 128, 128), 128)] = e.astype(jnp.bfloat16)
+            m, l = jnp.concatenate(ms, axis=1), jnp.concatenate(ls, axis=1)
+            mstat[pl.ds(c, 1), rows] = m
+            tops.append(m)
+            sums.append(l)
+
+        dots(0)
+        for c in range(n_chunk):
+            if c + 1 < n_chunk:
+                dots(c + 1)
+            soft(c)
+        top = functools.reduce(jnp.maximum, tops)
+        total = sum(l * jnp.exp2(m - top) for m, l in zip(tops, sums))
+        inner = pl.ds(pl.multiple_of(pid * block, block), block)
+        gath[cent, zj, 0:1, inner] = top
+        gath[cent, zj, 1:2, inner] = total
+
+        for at, jj in ((4, 0), (8, 1), (12, 2), (15, 3)):
+            @pl.when(n == at)
+            def _(jj=jj):
+                for d in range(1, NC):
+                    stat_copy(jj, d).start()
+        return 0
+
+    lax.fori_loop(0, 16, step, 0)
+
+    for d in range(1, NC):
+        frm = (cent + d) % NC
+        for w in range(NZ):
+            pltpu.make_async_remote_copy(
+                src_ref=gath.at[frm, w], dst_ref=gath.at[frm, w],
+                send_sem=stat_send.at[0, 0], recv_sem=stat_recv.at[frm, w],
+                device_id=sib, device_id_type=MESH,
+            ).wait_recv()
+    for w in range(NZ):
+        cols = slice(w * group, (w + 1) * group)
+        ms = [gath[q, w, 0:1, :] for q in range(NC)]
+        top = functools.reduce(jnp.maximum, ms)
+        total = sum(gath[q, w, 1:2, :] * jnp.exp2(ms[q] - top) for q in range(NC))
+        inv = 1.0 / total
+        for c in range(n_chunk):
+            scale_ref[c:c + 1, cols] = jnp.exp2(mstat[c:c + 1, cols] - top) * inv
+
+    sub = obuf.shape[2]
+    n_sub = CHUNK // sub
+
+    def out_copy(c, u):
+        col = pl.multiple_of(c * CHUNK + u * sub, sub)
+        return pltpu.make_async_copy(obuf.at[u], out_ref.at[:, pl.ds(col, sub)], out_sem.at[u])
+
+    def sums_step(c, _):
+        sc = scale_ref[pl.ds(c, 1), :]
+        a_ref[0:own_feats, :] = (xt_ref[...].astype(jnp.float32) * sc).astype(jnp.bfloat16)
+        hi = sc.astype(jnp.bfloat16).astype(jnp.float32)
+        lo = sc - hi
+        which = lax.broadcasted_iota(jnp.int32, (16, sc.shape[1]), 0)
+        extra = jnp.where(which == 0, hi, jnp.where(which == 1, lo, 0.0))
+        a_ref[own_feats:own_feats + 16, :] = extra.astype(jnp.bfloat16)
+        for u in range(n_sub):
+            ks = pl.ds(pl.multiple_of(c * CHUNK + u * sub, sub), sub)
+            res = lax.dot_general(a_ref[...], e_ref[ks, :], NT, preferred_element_type=jnp.float32)
+            counts = res[own_feats:own_feats + 1] + res[own_feats + 1:own_feats + 2]
+            inv = 1.0 / (counts + PRIOR)
+            own = c_ref[ks, own_col].astype(jnp.float32).T
+
+            @pl.when(c > 0)
+            def _(u=u):
+                out_copy(c - 1, u).wait()
+
+            obuf[u] = (res[:own_feats] + PRIOR * own) * inv
+            out_copy(c, u).start()
+        return 0
+
+    lax.fori_loop(0, n_chunk, sums_step, 0)
+    for u in range(n_sub):
+        out_copy(n_chunk - 1, u).wait()
+    for j in range(NZ):
+        for pos in POS:
+            each_route(j, pos, lambda c: c.wait_send())
+        for d in range(1, NC):
+            stat_copy(j, d).wait_send()
+
+
+def fused_local(points, centroids):
+    shard, feats = points.shape
+    kc = centroids.shape[0]
+    rows = shard * NZ * NC
+    own = feats // NZ
+    dma = pltpu.SemaphoreType.DMA
+    return pl.pallas_call(
+        fused,
+        out_shape=jax.ShapeDtypeStruct((own, kc), jnp.float32),
+        in_specs=[pl.BlockSpec(memory_space=pl.ANY)] * 2,
+        out_specs=pl.BlockSpec(memory_space=pl.ANY),
+        scratch_shapes=[
+            pltpu.VMEM((rows, feats), jnp.bfloat16),
+            pltpu.VMEM((kc, feats), jnp.bfloat16),
+            pltpu.VMEM((kc, rows), jnp.bfloat16),
+            pltpu.VMEM((own, rows), jnp.bfloat16),
+            pltpu.VMEM((own + 16, rows), jnp.bfloat16),
+            pltpu.VMEM((kc, 128), jnp.float32),
+            pltpu.VMEM((CHUNK, 2 * shard), jnp.float32),
+            pltpu.VMEM((CHUNK, 2 * shard), jnp.float32),
+            pltpu.VMEM((2, own, CHUNK // 2), jnp.float32),
+            pltpu.VMEM((kc // CHUNK, rows), jnp.float32),
+            pltpu.VMEM((kc // CHUNK, rows), jnp.float32),
+            pltpu.VMEM((NC, NZ, 2, NC * shard), jnp.float32),
+            dma((2,)),
+            dma((NZ * 4 * 5,)),
+            dma((NZ * NC,)),
+            dma((NZ, NC)),
+            dma((NC, NZ)),
+            dma((2,)),
+        ],
+        compiler_params=pltpu.CompilerParams(
+            collective_id=0, has_side_effects=True, vmem_limit_bytes=62 * 2**20
+        ),
+        cost_estimate=pl.CostEstimate(
+            flops=2 * rows * kc * (feats + own), bytes_accessed=2 * kc * feats + 4 * own * kc,
+            transcendentals=rows * kc,
+        ),
+    )(points, centroids)
 
 
 def solution(mesh):
+    def local(points, centroids):
+        small = (
+            mesh.shape["dp"] == NZ and mesh.shape["cent"] == NC
+            and points.shape == (128, 1024) and centroids.shape == (4096, 1024)
+        )
+        return fused_local(points, centroids) if small else general(points, centroids)
+
     return jax.shard_map(
         local,
         mesh=mesh,

time: 284 us -> 101 us (0.36)
  waiting for transfers between devices: 154 us -> 0 us
  Pallas kernels: 0 us -> 96 us
  blocking collectives: 44.1 us -> 0 us
  matrix products: 34.2 us -> 0 us
  other arithmetic: 31.6 us -> 0 us
  between operations: 13.5 us -> 0.01 us
    reduce_scatter x1 -> x0, waiting for transfers between devices: 126 us -> none  [local(): lax.psum_scatter(lax.dot_general(gathered, resp, (((0,), (0,)), ((), ()))...]
    pallas_call x0 -> x1, Pallas kernels: none -> 96 us  [fused_local(): pl.pallas_call(fused, out_shape=jax.ShapeDtypeStruct((own, kc), jnp.float...]
    dot_general x3 -> x0, matrix products: 34.2 us -> none  [the longest x2 22.9 us: logits_of(): lax.dot_general(xblock, centroids, (((1,), (1,)), ((), ())), preferred_el...]
    psum x2 -> x0, blocking collectives: 31 us -> none  [the longest x1 19 us: local(): counts_all = lax.psum(counts, 'dp')]
    all_gather x1 -> x0, waiting for transfers between devices: 27.5 us -> none  [local(): gathered = lax.all_gather(points, 'cent', axis=0, tiled=True)]
    reduce_sum x3 -> x0, other arithmetic: 21.1 us -> none  [the longest x1 8.1 us: local(): local_sum = jnp.sum(jnp.exp(logits - local_max[..., None]), axis=-1)]
    pmax x1 -> x0, blocking collectives: 13.1 us -> none  [local(): row_top = lax.pmax(local_max, 'cent')]
    reduce_max x1 -> x0, other arithmetic: 6.59 us -> none  [local(): local_max = jnp.max(logits, axis=-1)]
  transfers between devices with their start and end apart: 2 -> 0, of which waited for: 2 -> 0; matrix products, arithmetic and copies ran while one was open for 2% -> 0% of each run, Pallas kernels for 0% -> 0%
where the time goes in v1:
time: 101 us
  Pallas kernels  96 us (95%)
  local copies, waits for them, and re-layouts  4.65 us (5%)
    pallas_call x1, Pallas kernels, fused_local(): pl.pallas_call(fused, out_shape=jax.ShapeDtypeStruct((own, kc), jnp.float...  96 us
    unnamed x1, local copies, waits for them, and re-layouts  4.65 us

profile of v1, /device:TPU:0, one launch (start us, length us, event | category | flops | bytes accessed | tf_op | source)
XLA Modules:
  0.0 100.7 jit_solution(1112169825012726765)
XLA Ops:
  0.0 96.0 %shard_map.28 = f32[256,4096]{1,0:T(8,128)} custom-call(bf16[128,1024]{1,0:T(8,128)(2,1)} %points_ref.1, bf16[4096,1024]{1,0:T(8,128)(2,1)} %cents_ref.1), custom_call_target="tpu_custom_call" | custom-call | flops 42949672960 | bytes 12582912 | tf_op jit(solution)/shard_map/pallas_call | solution.py:335
  96.0 4.7 %copy.4 = f32[256,4096]{1,0:T(8,128)} copy(f32[256,4096]{1,0:T(8,128)} %shard_map.28) | data formatting | bytes 8388608

commit v2 on v1

--- a/solution.py
+++ b/solution.py
@@ -61,6 +61,7 @@
 
 NZ = 4
 NC = 8
+PIECE = 512
 CHUNK = 1024
 
 
@@ -175,7 +176,7 @@
     def norm_step(r, _):
         rows = pl.ds(pl.multiple_of(r * 256, 256), 256)
         v = c_ref[rows, :].astype(jnp.float32)
-        s = jnp.sum(v * v, axis=1, keepdims=True) * (0.5 * gain)
+        s = jnp.sum(v * v, axis=1, keepdims=True) * 0.5
         bias_ref[rows, :] = jnp.broadcast_to(s, (256, 128))
         return 0
 
@@ -191,12 +192,54 @@
 
     own_col = pl.ds(pl.multiple_of(z * own_feats, own_feats), own_feats)
     bufs = (buf0, buf1)
-
-    def step(n, _):
+    n_piece = CHUNK // PIECE
+    end = 1 - jnp.minimum(z, 1) * jnp.minimum(NZ - 1 - z, 1)
+
+    def top8(v):
+        return jnp.max(v.reshape(v.shape[0] // 8, 8, v.shape[1]), axis=0)
+
+    def dots(c, p, xb):
+        ks = slice(c * CHUNK + p * PIECE, c * CHUNK + (p + 1) * PIECE)
+        v = lax.dot_general(c_ref[ks, :], xb, NT, preferred_element_type=jnp.float32)
+        b = bias_ref[ks, :]
+        v = v - jnp.concatenate([b] * (block // 128), axis=1)
+        bufs[c % 2][p * PIECE:(p + 1) * PIECE, :] = v
+        return top8(v)
+
+    def expo(c, p, m, rows):
+        v = bufs[c % 2][p * PIECE:(p + 1) * PIECE, :]
+        e = jnp.exp2((v - m) * gain)
+        e_ref[c * CHUNK + p * PIECE:c * CHUNK + (p + 1) * PIECE, rows] = e.astype(jnp.bfloat16)
+        return jnp.sum(e.reshape(PIECE // 8, 8, block), axis=0)
+
+    def finish(zj, pid, tops, sums):
+        rows = pl.ds(pl.multiple_of(zj * group + pid * block, block), block)
+        for c in range(n_chunk):
+            mstat[c:c + 1, rows] = tops[c]
+        top = functools.reduce(jnp.maximum, tops)
+        total = sum(l * jnp.exp2((m - top) * gain) for m, l in zip(tops, sums))
+        inner = pl.ds(pl.multiple_of(pid * block, block), block)
+        gath[cent, zj, 0:1, inner] = top
+        gath[cent, zj, 1:2, inner] = total
+
+    def row_max(parts):
+        return jnp.max(functools.reduce(jnp.maximum, parts), axis=0, keepdims=True)
+
+    def row_sum(parts):
+        return jnp.sum(sum(parts), axis=0, keepdims=True)
+
+    def send_stats(j):
+        for d in range(1, NC):
+            stat_copy(j, d).start()
+
+    def step(n, carry):
+        pzj, ppid, ptops, psums = carry
         for at, items in (
             (1, ((0, "x"), (0, "y"), (1, "c"))),
-            (4, ((0, "d"), (1, "x"), (1, "y"), (2, "c"))),
-            (8, ((1, "d"), (2, "x"), (2, "y"), (3, "c"))),
+            (2 + 4 * end, ((2, "c"),)),
+            (4, ((0, "d"), (1, "x"), (1, "y"))),
+            (5 + 5 * end, ((3, "c"),)),
+            (8, ((1, "d"), (2, "x"), (2, "y"))),
             (12, ((2, "d"), (3, "x"), (3, "y"))),
             (15, ((3, "d"),)),
         ):
@@ -221,53 +264,41 @@
         px = xx + fx * (1 - 2 * xx)
         pid = py * 2 + px
         wait_piece(zj * NC + pid * 2 + 1 - core)
-        row = pl.multiple_of(zj * group + pid * block, block)
-        rows = pl.ds(row, block)
+        rows = pl.ds(pl.multiple_of(zj * group + pid * block, block), block)
+        prows = pl.ds(pl.multiple_of(pzj * group + ppid * block, block), block)
         xb = x_ref[rows, :]
-        xt_ref[:, rows] = x_ref[rows, own_col].astype(jnp.float32).T.astype(jnp.bfloat16)
-
-        def dots(c):
-            bufs[c % 2][...] = lax.dot_general(
-                c_ref[c * CHUNK:(c + 1) * CHUNK, :], xb, NT, preferred_element_type=jnp.float32
-            )
 
         tops, sums = [], []
-
-        def soft(c):
-            ks = slice(c * CHUNK, (c + 1) * CHUNK)
-            b = bias_ref[ks, :]
-            ms, ls = [], []
-            for h in range(block // 128):
-                t = bufs[c % 2][:, h * 128:(h + 1) * 128] * gain - b
-                m = jnp.max(t, axis=0, keepdims=True)
-                e = jnp.exp2(t - m)
-                ls.append(jnp.sum(e, axis=0, keepdims=True))
-                ms.append(m)
-                e_ref[ks, pl.ds(pl.multiple_of(row + h * 128, 128), 128)] = e.astype(jnp.bfloat16)
-            m, l = jnp.concatenate(ms, axis=1), jnp.concatenate(ls, axis=1)
-            mstat[pl.ds(c, 1), rows] = m
+        m, where = ptops[-1], prows
+        for c in range(n_chunk):
+            t8, s8 = [], []
+            for p in range(n_piece):
+                t8.append(dots(c, p, xb))
+                s8.append(expo((c - 1) % n_chunk, p, m, where))
+            if c == 0:
+                finish(pzj, ppid, ptops, list(psums) + [row_sum(s8)])
+                xt_ref[:, rows] = x_ref[rows, own_col].astype(jnp.float32).T.astype(jnp.bfloat16)
+            else:
+                sums.append(row_sum(s8))
+            m, where = row_max(t8), rows
             tops.append(m)
-            sums.append(l)
-
-        dots(0)
-        for c in range(n_chunk):
-            if c + 1 < n_chunk:
-                dots(c + 1)
-            soft(c)
-        top = functools.reduce(jnp.maximum, tops)
-        total = sum(l * jnp.exp2(m - top) for m, l in zip(tops, sums))
-        inner = pl.ds(pl.multiple_of(pid * block, block), block)
-        gath[cent, zj, 0:1, inner] = top
-        gath[cent, zj, 1:2, inner] = total
-
-        for at, jj in ((4, 0), (8, 1), (12, 2), (15, 3)):
+
+        for at, jj in ((5, 0), (9, 1), (13, 2)):
             @pl.when(n == at)
             def _(jj=jj):
-                for d in range(1, NC):
-                    stat_copy(jj, d).start()
-        return 0
-
-    lax.fori_loop(0, 16, step, 0)
+                send_stats(jj)
+        return zj, pid, tuple(tops), tuple(sums)
+
+    last_buf = bufs[(n_chunk - 1) % 2]
+    last_buf[...] = jnp.zeros_like(last_buf)
+    zero = jnp.zeros((1, block), jnp.float32)
+    pzj, ppid, ptops, psums = lax.fori_loop(
+        0, 16, step, (z, yy * 2 + xx, (zero,) * n_chunk, (zero,) * (n_chunk - 1))
+    )
+    prows = pl.ds(pl.multiple_of(pzj * group + ppid * block, block), block)
+    s8 = [expo(n_chunk - 1, p, ptops[-1], prows) for p in range(n_piece)]
+    finish(pzj, ppid, ptops, list(psums) + [row_sum(s8)])
+    send_stats(3)
 
     for d in range(1, NC):
         frm = (cent + d) % NC
@@ -281,10 +312,10 @@
         cols = slice(w * group, (w + 1) * group)
         ms = [gath[q, w, 0:1, :] for q in range(NC)]
         top = functools.reduce(jnp.maximum, ms)
-        total = sum(gath[q, w, 1:2, :] * jnp.exp2(ms[q] - top) for q in range(NC))
+        total = sum(gath[q, w, 1:2, :] * jnp.exp2((ms[q] - top) * gain) for q in range(NC))
         inv = 1.0 / total
         for c in range(n_chunk):
-            scale_ref[c:c + 1, cols] = jnp.exp2(mstat[c:c + 1, cols] - top) * inv
+            scale_ref[c:c + 1, cols] = jnp.exp2((mstat[c:c + 1, cols] - top) * gain) * inv
 
     sub = obuf.shape[2]
     n_sub = CHUNK // sub

time: 101 us -> 88.3 us (0.87)
  Pallas kernels: 96 us -> 83.5 us
    pallas_call x1, Pallas kernels: 96 us -> 83.5 us  [fused_local(): pl.pallas_call(fused, out_shape=jax.ShapeDtypeStruct((own, kc), jnp.float...]
where the time goes in v2:
time: 88.3 us; the launch traced here: 88.2 us
  Pallas kernels  83.5 us (95%)
  local copies, waits for them, and re-layouts  4.65 us (5%)
    pallas_call x1, Pallas kernels, fused_local(): pl.pallas_call(fused, out_shape=jax.ShapeDtypeStruct((own, kc), jnp.float...  83.5 us
    unnamed x1, local copies, waits for them, and re-layouts  4.65 us

profile of v2, /device:TPU:0, one launch (start us, length us, event | category | flops | bytes accessed | tf_op | source)
XLA Modules:
  0.0 88.2 jit_solution(7517893315351450010)
XLA Ops:
  0.0 83.5 %shard_map.28 = f32[256,4096]{1,0:T(8,128)} custom-call(bf16[128,1024]{1,0:T(8,128)(2,1)} %points_ref.1, bf16[4096,1024]{1,0:T(8,128)(2,1)} %cents_ref.1), custom_call_target="tpu_custom_call" | custom-call | flops 42949672960 | bytes 12582912 | tf_op jit(solution)/shard_map/pallas_call | solution.py:366
  83.5 4.7 %copy.4 = f32[256,4096]{1,0:T(8,128)} copy(f32[256,4096]{1,0:T(8,128)} %shard_map.28) | data formatting | bytes 8388608

commit v3 on v2

--- a/solution.py
+++ b/solution.py
@@ -67,12 +67,13 @@
 
 def fused(
     points_ref, cents_ref, out_ref,
-    x_ref, c_ref, e_ref, xt_ref, a_ref, bias_ref, buf0, buf1, obuf, mstat, scale_ref, gath,
-    load_sem, send_sem, recv_sem, stat_send, stat_recv, out_sem,
+    x_ref, c_ref, far_ref, e_ref, xt_ref, a0_ref, a1_ref, bias_ref, buf0, buf1, buf2, obuf,
+    mstat, scale_ref, gath, lone, nsend, nrecv, csend, crecv,
+    load_sem, send_sem, recv_sem, stat_send, stat_recv, pair_send, pair_recv, out_sem,
 ):
     shard, feats = points_ref.shape
-    kc = cents_ref.shape[0]
-    n_chunk = kc // CHUNK
+    n_chunk = cents_ref.shape[0] // CHUNK - 1
+    kc = n_chunk * CHUNK
     block = 2 * shard
     group = NC * shard
     own_feats = feats // NZ
@@ -84,6 +85,10 @@
     xx = (cent // 2) % 2
     yy = cent // 4
     flip = z // 2
+    odd = z % 2
+    pz = z + 1 - 2 * odd
+    lone_row = pl.multiple_of(odd * kc, CHUNK)
+    far_row = pl.multiple_of((1 - odd) * kc, CHUNK)
     zz = z + flip * (3 - 2 * z)
 
     def z_of(j):
@@ -151,27 +156,40 @@
 
     own_id = sid_of(0, "c")
     load_x = pltpu.make_async_copy(points_ref, piece(own_id), load_sem.at[0])
-    load_c = pltpu.make_async_copy(cents_ref, c_ref, load_sem.at[1])
+    own_col = pl.ds(pl.multiple_of(z * own_feats, own_feats), own_feats)
+    pair_col = pl.ds(pl.multiple_of(pz * own_feats, own_feats), own_feats)
+    loads = [
+        pltpu.make_async_copy(
+            cents_ref.at[pl.ds(lone_row, CHUNK)], c_ref.at[pl.ds(0, CHUNK)], load_sem.at[1]
+        ),
+        pltpu.make_async_copy(
+            cents_ref.at[pl.ds(CHUNK, kc - CHUNK)], c_ref.at[pl.ds(CHUNK, kc - CHUNK)],
+            load_sem.at[2],
+        ),
+        pltpu.make_async_copy(
+            cents_ref.at[pl.ds(far_row, CHUNK), own_col], far_ref, load_sem.at[3]
+        ),
+    ]
     load_x.start()
-    load_c.start()
+    for c in loads:
+        c.start()
     barrier = pltpu.get_barrier_semaphore()
     for d in range(1, NC):
         pl.semaphore_signal(barrier, inc=1, device_id=(z, (cent + d) % NC), device_id_type=MESH)
-
-    @pl.when(z > 0)
+    for d in range(NC):
+        pl.semaphore_signal(barrier, inc=1, device_id=(pz, (cent + d) % NC), device_id_type=MESH)
+    inner_z = jnp.minimum(z, 1) * jnp.minimum(NZ - 1 - z, 1)
+
+    @pl.when(inner_z == 1)
     def _():
-        pl.semaphore_signal(barrier, inc=1, device_id=(z - 1, cent), device_id_type=MESH)
-
-    @pl.when(z < NZ - 1)
-    def _():
-        pl.semaphore_signal(barrier, inc=1, device_id=(z + 1, cent), device_id_type=MESH)
-
-    inner_z = jnp.minimum(z, 1) * jnp.minimum(NZ - 1 - z, 1)
-    pl.semaphore_wait(barrier, NC + inner_z)
+        pl.semaphore_signal(barrier, inc=1, device_id=(3 - z, cent), device_id_type=MESH)
+
+    pl.semaphore_wait(barrier, 2 * NC - 1 + inner_z)
 
     load_x.wait()
     pass_on(0, "c")
-    load_c.wait()
+    for c in loads:
+        c.wait()
 
     def norm_step(r, _):
         rows = pl.ds(pl.multiple_of(r * 256, 256), 256)
@@ -184,16 +202,19 @@
 
     def stat_copy(j, d):
         zj = z_of(j)
+        if d < NC:
+            src, slot, dev = gath.at[cent, zj], cent, (z, (cent + d) % NC)
+        else:
+            src, slot, dev = lone.at[zj], cent + NC, (pz, (cent + d) % NC)
         return pltpu.make_async_remote_copy(
-            src_ref=gath.at[cent, zj], dst_ref=gath.at[cent, zj],
-            send_sem=stat_send.at[j, d], recv_sem=stat_recv.at[cent, zj],
-            device_id=(z, (cent + d) % NC), device_id_type=MESH,
-        )
-
-    own_col = pl.ds(pl.multiple_of(z * own_feats, own_feats), own_feats)
-    bufs = (buf0, buf1)
+            src_ref=src, dst_ref=gath.at[slot, zj],
+            send_sem=stat_send.at[j, d], recv_sem=stat_recv.at[slot, zj],
+            device_id=dev, device_id_type=MESH,
+        )
+
+    bufs = (buf0, buf1, buf2)
     n_piece = CHUNK // PIECE
-    end = 1 - jnp.minimum(z, 1) * jnp.minimum(NZ - 1 - z, 1)
+    end = 1 - inner_z
 
     def top8(v):
         return jnp.max(v.reshape(v.shape[0] // 8, 8, v.shape[1]), axis=0)
@@ -203,11 +224,11 @@
         v = lax.dot_general(c_ref[ks, :], xb, NT, preferred_element_type=jnp.float32)
         b = bias_ref[ks, :]
         v = v - jnp.concatenate([b] * (block // 128), axis=1)
-        bufs[c % 2][p * PIECE:(p + 1) * PIECE, :] = v
+        bufs[c][p * PIECE:(p + 1) * PIECE, :] = v
         return top8(v)
 
     def expo(c, p, m, rows):
-        v = bufs[c % 2][p * PIECE:(p + 1) * PIECE, :]
+        v = bufs[c][p * PIECE:(p + 1) * PIECE, :]
         e = jnp.exp2((v - m) * gain)
         e_ref[c * CHUNK + p * PIECE:c * CHUNK + (p + 1) * PIECE, rows] = e.astype(jnp.bfloat16)
         return jnp.sum(e.reshape(PIECE // 8, 8, block), axis=0)
@@ -221,6 +242,8 @@
         inner = pl.ds(pl.multiple_of(pid * block, block), block)
         gath[cent, zj, 0:1, inner] = top
         gath[cent, zj, 1:2, inner] = total
+        lone[zj, 0:1, inner] = tops[0]
+        lone[zj, 1:2, inner] = sums[0]
 
     def row_max(parts):
         return jnp.max(functools.reduce(jnp.maximum, parts), axis=0, keepdims=True)
@@ -229,7 +252,7 @@
         return jnp.sum(sum(parts), axis=0, keepdims=True)
 
     def send_stats(j):
-        for d in range(1, NC):
+        for d in range(1, 2 * NC):
             stat_copy(j, d).start()
 
     def step(n, carry):
@@ -277,7 +300,9 @@
                 s8.append(expo((c - 1) % n_chunk, p, m, where))
             if c == 0:
                 finish(pzj, ppid, ptops, list(psums) + [row_sum(s8)])
-                xt_ref[:, rows] = x_ref[rows, own_col].astype(jnp.float32).T.astype(jnp.bfloat16)
+                for half, cols in enumerate((own_col, pair_col)):
+                    xt = x_ref[rows, cols].astype(jnp.float32).T.astype(jnp.bfloat16)
+                    xt_ref[half * own_feats:(half + 1) * own_feats, rows] = xt
             else:
                 sums.append(row_sum(s8))
             m, where = row_max(t8), rows
@@ -289,7 +314,7 @@
                 send_stats(jj)
         return zj, pid, tuple(tops), tuple(sums)
 
-    last_buf = bufs[(n_chunk - 1) % 2]
+    last_buf = bufs[n_chunk - 1]
     last_buf[...] = jnp.zeros_like(last_buf)
     zero = jnp.zeros((1, block), jnp.float32)
     pzj, ppid, ptops, psums = lax.fori_loop(
@@ -300,8 +325,8 @@
     finish(pzj, ppid, ptops, list(psums) + [row_sum(s8)])
     send_stats(3)
 
-    for d in range(1, NC):
-        frm = (cent + d) % NC
+    for d in range(1, 2 * NC):
+        frm = (cent + d) % NC + (NC if d >= NC else 0)
         for w in range(NZ):
             pltpu.make_async_remote_copy(
                 src_ref=gath.at[frm, w], dst_ref=gath.at[frm, w],
@@ -310,83 +335,145 @@
             ).wait_recv()
     for w in range(NZ):
         cols = slice(w * group, (w + 1) * group)
-        ms = [gath[q, w, 0:1, :] for q in range(NC)]
+        ms = [gath[q, w, 0:1, :] for q in range(2 * NC)]
         top = functools.reduce(jnp.maximum, ms)
-        total = sum(gath[q, w, 1:2, :] * jnp.exp2((ms[q] - top) * gain) for q in range(NC))
+        total = sum(
+            gath[q, w, 1:2, :] * jnp.exp2((ms[q] - top) * gain) for q in range(2 * NC)
+        )
         inv = 1.0 / total
         for c in range(n_chunk):
             scale_ref[c:c + 1, cols] = jnp.exp2((mstat[c:c + 1, cols] - top) * gain) * inv
 
     sub = obuf.shape[2]
     n_sub = CHUNK // sub
-
-    def out_copy(c, u):
-        col = pl.multiple_of(c * CHUNK + u * sub, sub)
-        return pltpu.make_async_copy(obuf.at[u], out_ref.at[:, pl.ds(col, sub)], out_sem.at[u])
-
-    def sums_step(c, _):
-        sc = scale_ref[pl.ds(c, 1), :]
-        a_ref[0:own_feats, :] = (xt_ref[...].astype(jnp.float32) * sc).astype(jnp.bfloat16)
+    slots = obuf.shape[0]
+    a_refs = (a0_ref, a1_ref)
+    writes = []
+
+    def write(value, row):
+        t = len(writes)
+        if t >= slots:
+            writes[t - slots].wait()
+        obuf[t % slots] = value
+        copy = pltpu.make_async_copy(
+            obuf.at[t % slots], out_ref.at[:, pl.ds(row, sub)], out_sem.at[t % slots]
+        )
+        copy.start()
+        writes.append(copy)
+
+    def pair_copies(u):
+        return [
+            pltpu.make_async_remote_copy(
+                src_ref=src.at[u], dst_ref=dst.at[u], send_sem=pair_send.at[i, u],
+                recv_sem=pair_recv.at[i, u], device_id=(pz, cent), device_id_type=MESH,
+            )
+            for i, (src, dst) in enumerate(((nsend, nrecv), (csend, crecv)))
+        ]
+
+    def prepare(c):
+        feats_here = own_feats * (2 if c == 0 else 1)
+        a = a_refs[c % 2]
+        sc = scale_ref[c:c + 1, :]
+        a[0:feats_here, :] = (xt_ref[0:feats_here, :].astype(jnp.float32) * sc).astype(jnp.bfloat16)
         hi = sc.astype(jnp.bfloat16).astype(jnp.float32)
-        lo = sc - hi
         which = lax.broadcasted_iota(jnp.int32, (16, sc.shape[1]), 0)
-        extra = jnp.where(which == 0, hi, jnp.where(which == 1, lo, 0.0))
-        a_ref[own_feats:own_feats + 16, :] = extra.astype(jnp.bfloat16)
+        extra = jnp.where(which == 0, hi, jnp.where(which == 1, sc - hi, 0.0))
+        a[feats_here:feats_here + 16, :] = extra.astype(jnp.bfloat16)
+
+    def multiply(c, u):
+        height = own_feats * (2 if c == 0 else 1)
+        ks = slice(c * CHUNK + u * sub, c * CHUNK + (u + 1) * sub)
+        res = lax.dot_general(
+            a_refs[c % 2][0:height + 16, :], e_ref[ks, :], NT, preferred_element_type=jnp.float32
+        )
+        counts = res[height:height + 1] + res[height + 1:height + 2]
+        if c == 0:
+            nsend[u] = res[own_feats:height].astype(jnp.bfloat16)
+            csend[u] = jnp.broadcast_to(counts, csend.shape[1:])
+            for copy in pair_copies(u):
+                copy.start()
+        return res[:own_feats], counts
+
+    def conclude(c, u, numer, counts):
+        ks = slice(c * CHUNK + u * sub, c * CHUNK + (u + 1) * sub)
+        own = c_ref[ks, own_col].astype(jnp.float32).T
+        base = lone_row if c == 0 else c * CHUNK
+        write((numer + PRIOR * own) * (1.0 / (counts + PRIOR)), base + u * sub)
+
+    prepare(0)
+    pending = None
+    for c in range(n_chunk):
         for u in range(n_sub):
-            ks = pl.ds(pl.multiple_of(c * CHUNK + u * sub, sub), sub)
-            res = lax.dot_general(a_ref[...], e_ref[ks, :], NT, preferred_element_type=jnp.float32)
-            counts = res[own_feats:own_feats + 1] + res[own_feats + 1:own_feats + 2]
-            inv = 1.0 / (counts + PRIOR)
-            own = c_ref[ks, own_col].astype(jnp.float32).T
-
-            @pl.when(c > 0)
-            def _(u=u):
-                out_copy(c - 1, u).wait()
-
-            obuf[u] = (res[:own_feats] + PRIOR * own) * inv
-            out_copy(c, u).start()
-        return 0
-
-    lax.fori_loop(0, n_chunk, sums_step, 0)
+            done = multiply(c, u)
+            if u == 0 and c + 1 < n_chunk:
+                prepare(c + 1)
+            if pending is not None:
+                conclude(*pending)
+            pending = (c, u, *done)
+    conclude(*pending)
     for u in range(n_sub):
-        out_copy(n_chunk - 1, u).wait()
+        for copy in pair_copies(u):
+            copy.wait_recv()
+        own = far_ref[u * sub:(u + 1) * sub, :].astype(jnp.float32).T
+        counts = crecv[u][0:1]
+        write(
+            (nrecv[u].astype(jnp.float32) + PRIOR * own) * (1.0 / (counts + PRIOR)),
+            pl.multiple_of(far_row + u * sub, sub),
+        )
+    for copy in writes[-slots:]:
+        copy.wait()
+    for u in range(n_sub):
+        for copy in pair_copies(u):
+            copy.wait_send()
     for j in range(NZ):
         for pos in POS:
             each_route(j, pos, lambda c: c.wait_send())
-        for d in range(1, NC):
+        for d in range(1, 2 * NC):
             stat_copy(j, d).wait_send()
 
 
 def fused_local(points, centroids):
     shard, feats = points.shape
-    kc = centroids.shape[0]
+    all_kc = centroids.shape[0]
+    kc = all_kc - CHUNK
+    half = CHUNK // 2
     rows = shard * NZ * NC
     own = feats // NZ
     dma = pltpu.SemaphoreType.DMA
     return pl.pallas_call(
         fused,
-        out_shape=jax.ShapeDtypeStruct((own, kc), jnp.float32),
+        out_shape=jax.ShapeDtypeStruct((own, all_kc), jnp.float32),
         in_specs=[pl.BlockSpec(memory_space=pl.ANY)] * 2,
         out_specs=pl.BlockSpec(memory_space=pl.ANY),
         scratch_shapes=[
             pltpu.VMEM((rows, feats), jnp.bfloat16),
             pltpu.VMEM((kc, feats), jnp.bfloat16),
+            pltpu.VMEM((CHUNK, own), jnp.bfloat16),
             pltpu.VMEM((kc, rows), jnp.bfloat16),
-            pltpu.VMEM((own, rows), jnp.bfloat16),
+            pltpu.VMEM((2 * own, rows), jnp.bfloat16),
+            pltpu.VMEM((2 * own + 16, rows), jnp.bfloat16),
             pltpu.VMEM((own + 16, rows), jnp.bfloat16),
             pltpu.VMEM((kc, 128), jnp.float32),
             pltpu.VMEM((CHUNK, 2 * shard), jnp.float32),
             pltpu.VMEM((CHUNK, 2 * shard), jnp.float32),
-            pltpu.VMEM((2, own, CHUNK // 2), jnp.float32),
+            pltpu.VMEM((CHUNK, 2 * shard), jnp.float32),
+            pltpu.VMEM((4, own, half), jnp.float32),
             pltpu.VMEM((kc // CHUNK, rows), jnp.float32),
             pltpu.VMEM((kc // CHUNK, rows), jnp.float32),
-            pltpu.VMEM((NC, NZ, 2, NC * shard), jnp.float32),
-            dma((2,)),
+            pltpu.VMEM((2 * NC, NZ, 2, NC * shard), jnp.float32),
+            pltpu.VMEM((NZ, 2, NC * shard), jnp.float32),
+            pltpu.VMEM((2, own, half), jnp.bfloat16),
+            pltpu.VMEM((2, own, half), jnp.bfloat16),
+            pltpu.VMEM((2, 8, half), jnp.float32),
+            pltpu.VMEM((2, 8, half), jnp.float32),
+            dma((4,)),
             dma((NZ * 4 * 5,)),
             dma((NZ * NC,)),
-            dma((NZ, NC)),
-            dma((NC, NZ)),
-            dma((2,)),
+            dma((NZ, 2 * NC)),
+            dma((2 * NC, NZ)),
+            dma((2, 2)),
+            dma((2, 2)),
+            dma((4,)),
         ],
         compiler_params=pltpu.CompilerParams(
             collective_id=0, has_side_effects=True, vmem_limit_bytes=62 * 2**20

time: 88.3 us -> 91.6 us (1.037)
  Pallas kernels: 83.5 us -> 86.8 us
    pallas_call x1, Pallas kernels: 83.5 us -> 86.8 us  [fused_local(): pl.pallas_call(fused, out_shape=jax.ShapeDtypeStruct((own, all_kc), jnp.f...]
where the time goes in v3:
time: 91.6 us; the launch traced here: 91.4 us
  Pallas kernels  86.8 us (95%)
  local copies, waits for them, and re-layouts  4.65 us (5%)
    pallas_call x1, Pallas kernels, fused_local(): pl.pallas_call(fused, out_shape=jax.ShapeDtypeStruct((own, all_kc), jnp.f...  86.8 us
    unnamed x1, local copies, waits for them, and re-layouts  4.65 us

profile of v3, /device:TPU:0, one launch (start us, length us, event | category | flops | bytes accessed | tf_op | source)
XLA Modules:
  0.0 91.4 jit_solution(5396889065094495589)
XLA Ops:
  0.0 86.8 %shard_map.28 = f32[256,4096]{1,0:T(8,128)} custom-call(bf16[128,1024]{1,0:T(8,128)(2,1)} %points_ref.1, bf16[4096,1024]{1,0:T(8,128)(2,1)} %cents_ref.1), custom_call_target="tpu_custom_call" | custom-call | flops 32212254720 | bytes 9437184 | tf_op jit(solution)/shard_map/pallas_call | solution.py:443
  86.8 4.7 %copy.4 = f32[256,4096]{1,0:T(8,128)} copy(f32[256,4096]{1,0:T(8,128)} %shard_map.28) | data formatting | bytes 8388608

commit v4 on v3

--- a/solution.py
+++ b/solution.py
@@ -65,6 +65,22 @@
 CHUNK = 1024
 
 
+ORDER = (
+    "c0", "x0", "y0", "c1", "x1", "c2", "y1", "d0",
+    "x2", "c3", "y2", "x3", "d1", "y3", "d2", "d3",
+)
+DIGITS = tuple(
+    tuple(
+        sum(f(b) << (2 * i) for i, b in enumerate(ORDER[h:h + 8])) for h in (0, 8)
+    )
+    for f in (lambda b: int(b[1]), lambda b: int(b[0] in "xd"), lambda b: int(b[0] in "yd"))
+)
+
+
+def order_digit(k, n):
+    return (jnp.where(n < 8, DIGITS[k][0], DIGITS[k][1]) >> (2 * (n % 8))) % 4
+
+
 def fused(
     points_ref, cents_ref, out_ref,
     x_ref, c_ref, far_ref, e_ref, xt_ref, a0_ref, a1_ref, bias_ref, buf0, buf1, buf2, obuf,
@@ -259,26 +275,21 @@
         pzj, ppid, ptops, psums = carry
         for at, items in (
             (1, ((0, "x"), (0, "y"), (1, "c"))),
-            (2 + 4 * end, ((2, "c"),)),
-            (4, ((0, "d"), (1, "x"), (1, "y"))),
-            (5 + 5 * end, ((3, "c"),)),
-            (8, ((1, "d"), (2, "x"), (2, "y"))),
-            (12, ((2, "d"), (3, "x"), (3, "y"))),
-            (15, ((3, "d"),)),
+            (1 + 2 * end, ((2, "c"),)),
+            (3, ((1, "x"),)),
+            (3 + 2 * end, ((3, "c"),)),
+            (5, ((1, "y"), (0, "d"), (2, "x"))),
+            (7, ((2, "y"),)),
+            (9, ((3, "x"), (1, "d"))),
+            (11, ((3, "y"), (2, "d"))),
+            (14, ((3, "d"),)),
         ):
             @pl.when(n == at)
             def _(items=items):
                 for j, pos in items:
                     pass_on(j, pos)
 
-        g, r = n // 4, n % 4
-        last = n // 15
-        first = 1 - jnp.minimum(n, 1)
-        r0 = 1 - jnp.minimum(r, 1)
-        r3 = r // 3
-        j = g - r0 + first + r3 - last
-        fx = jnp.where(r == 1, 1, 0) + r0 - first + last
-        fy = jnp.where(r == 2, 1, 0) + r0 - first + last
+        j, fx, fy = (order_digit(k, n) for k in range(3))
         j1 = jnp.where(j == 1, 1, 0)
         j0 = jnp.where(j == 0, 1, 0)
         s = j0 * zz + j1 * (1 - zz) + (1 - j0 - j1) * j
@@ -308,7 +319,7 @@
             m, where = row_max(t8), rows
             tops.append(m)
 
-        for at, jj in ((5, 0), (9, 1), (13, 2)):
+        for at, jj in ((8, 0), (13, 1), (15, 2)):
             @pl.when(n == at)
             def _(jj=jj):
                 send_stats(jj)

time: 91.6 us -> 86 us (0.939)
  Pallas kernels: 86.8 us -> 81.2 us
    pallas_call x1, Pallas kernels: 86.8 us -> 81.2 us  [fused_local(): pl.pallas_call(fused, out_shape=jax.ShapeDtypeStruct((own, all_kc), jnp.f...]
where the time goes in v4:
time: 86 us; the launch traced here: 85.8 us
  Pallas kernels  81.2 us (94%)
  local copies, waits for them, and re-layouts  4.65 us (5%)
    pallas_call x1, Pallas kernels, fused_local(): pl.pallas_call(fused, out_shape=jax.ShapeDtypeStruct((own, all_kc), jnp.f...  81.2 us
    unnamed x1, local copies, waits for them, and re-layouts  4.65 us

profile of v4, /device:TPU:0, one launch (start us, length us, event | category | flops | bytes accessed | tf_op | source)
XLA Modules:
  0.0 85.8 jit_solution(10836856964770021085)
XLA Ops:
  0.0 81.2 %shard_map.28 = f32[256,4096]{1,0:T(8,128)} custom-call(bf16[128,1024]{1,0:T(8,128)(2,1)} %points_ref.1, bf16[4096,1024]{1,0:T(8,128)(2,1)} %cents_ref.1), custom_call_target="tpu_custom_call" | custom-call | flops 32212254720 | bytes 9437184 | tf_op jit(solution)/shard_map/pallas_call | solution.py:454
  81.2 4.7 %copy.4 = f32[256,4096]{1,0:T(8,128)} copy(f32[256,4096]{1,0:T(8,128)} %shard_map.28) | data formatting | bytes 8388608

commit v5 on v4

--- a/solution.py
+++ b/solution.py
@@ -83,8 +83,8 @@
 
 def fused(
     points_ref, cents_ref, out_ref,
-    x_ref, c_ref, far_ref, e_ref, xt_ref, a0_ref, a1_ref, bias_ref, buf0, buf1, buf2, obuf,
-    mstat, scale_ref, gath, lone, nsend, nrecv, csend, crecv,
+    x_ref, c_ref, far_ref, e_ref, a0_ref, a1_ref, bias_ref, buf0, buf1, buf2, obuf,
+    mstat, scale_ref, scale_t, gath, lone, nsend, nrecv, csend, crecv,
     load_sem, send_sem, recv_sem, stat_send, stat_recv, pair_send, pair_recv, out_sem,
 ):
     shard, feats = points_ref.shape
@@ -311,9 +311,6 @@
                 s8.append(expo((c - 1) % n_chunk, p, m, where))
             if c == 0:
                 finish(pzj, ppid, ptops, list(psums) + [row_sum(s8)])
-                for half, cols in enumerate((own_col, pair_col)):
-                    xt = x_ref[rows, cols].astype(jnp.float32).T.astype(jnp.bfloat16)
-                    xt_ref[half * own_feats:(half + 1) * own_feats, rows] = xt
             else:
                 sums.append(row_sum(s8))
             m, where = row_max(t8), rows
@@ -344,6 +341,7 @@
                 send_sem=stat_send.at[0, 0], recv_sem=stat_recv.at[frm, w],
                 device_id=sib, device_id_type=MESH,
             ).wait_recv()
+    scale_ref[...] = jnp.zeros_like(scale_ref)
     for w in range(NZ):
         cols = slice(w * group, (w + 1) * group)
         ms = [gath[q, w, 0:1, :] for q in range(2 * NC)]
@@ -381,29 +379,34 @@
             for i, (src, dst) in enumerate(((nsend, nrecv), (csend, crecv)))
         ]
 
+    scale_t[...] = scale_ref[...].T
+
     def prepare(c):
-        feats_here = own_feats * (2 if c == 0 else 1)
-        a = a_refs[c % 2]
-        sc = scale_ref[c:c + 1, :]
-        a[0:feats_here, :] = (xt_ref[0:feats_here, :].astype(jnp.float32) * sc).astype(jnp.bfloat16)
-        hi = sc.astype(jnp.bfloat16).astype(jnp.float32)
-        which = lax.broadcasted_iota(jnp.int32, (16, sc.shape[1]), 0)
-        extra = jnp.where(which == 0, hi, jnp.where(which == 1, sc - hi, 0.0))
-        a[feats_here:feats_here + 16, :] = extra.astype(jnp.bfloat16)
+        for half, cols in enumerate((own_col, pair_col) if c == 0 else (own_col,)):
+            scaled = x_ref[:, cols].astype(jnp.float32) * scale_t[:, c:c + 1]
+            a_refs[c % 2][:, half * own_feats:(half + 1) * own_feats] = scaled.astype(jnp.bfloat16)
 
     def multiply(c, u):
-        height = own_feats * (2 if c == 0 else 1)
+        width = own_feats * (2 if c == 0 else 1)
         ks = slice(c * CHUNK + u * sub, c * CHUNK + (u + 1) * sub)
-        res = lax.dot_general(
-            a_refs[c % 2][0:height + 16, :], e_ref[ks, :], NT, preferred_element_type=jnp.float32
-        )
-        counts = res[height:height + 1] + res[height + 1:height + 2]
+        res = jnp.dot(
+            e_ref[ks, :], a_refs[c % 2][:, 0:width], preferred_element_type=jnp.float32
+        )
+        parts = []
+        for r in range(ks.start, ks.stop, 128):
+            acc = jnp.zeros((128, 128), jnp.float32)
+            for i in range(0, e_ref.shape[1], 128):
+                e = e_ref[r:r + 128, i:i + 128].astype(jnp.float32)
+                acc = acc + e * scale_ref[c:c + 1, i:i + 128]
+            parts.append(jnp.sum(acc, axis=1, keepdims=True))
+        counts = jnp.concatenate(parts, axis=0)
+        counts = jnp.broadcast_to(counts, (sub, 128)).T[0:8]
         if c == 0:
-            nsend[u] = res[own_feats:height].astype(jnp.bfloat16)
-            csend[u] = jnp.broadcast_to(counts, csend.shape[1:])
+            nsend[u] = res[:, own_feats:].T.astype(jnp.bfloat16)
+            csend[u] = counts
             for copy in pair_copies(u):
                 copy.start()
-        return res[:own_feats], counts
+        return res[:, :own_feats].T, counts[0:1]
 
     def conclude(c, u, numer, counts):
         ks = slice(c * CHUNK + u * sub, c * CHUNK + (u + 1) * sub)
@@ -461,16 +464,16 @@
             pltpu.VMEM((kc, feats), jnp.bfloat16),
             pltpu.VMEM((CHUNK, own), jnp.bfloat16),
             pltpu.VMEM((kc, rows), jnp.bfloat16),
-            pltpu.VMEM((2 * own, rows), jnp.bfloat16),
-            pltpu.VMEM((2 * own + 16, rows), jnp.bfloat16),
-            pltpu.VMEM((own + 16, rows), jnp.bfloat16),
+            pltpu.VMEM((rows, 2 * own), jnp.bfloat16),
+            pltpu.VMEM((rows, own), jnp.bfloat16),
             pltpu.VMEM((kc, 128), jnp.float32),
             pltpu.VMEM((CHUNK, 2 * shard), jnp.float32),
             pltpu.VMEM((CHUNK, 2 * shard), jnp.float32),
             pltpu.VMEM((CHUNK, 2 * shard), jnp.float32),
             pltpu.VMEM((4, own, half), jnp.float32),
             pltpu.VMEM((kc // CHUNK, rows), jnp.float32),
-            pltpu.VMEM((kc // CHUNK, rows), jnp.float32),
+            pltpu.VMEM((8, rows), jnp.float32),
+            pltpu.VMEM((rows, 8), jnp.float32),
             pltpu.VMEM((2 * NC, NZ, 2, NC * shard), jnp.float32),
             pltpu.VMEM((NZ, 2, NC * shard), jnp.float32),
             pltpu.VMEM((2, own, half), jnp.bfloat16),

time: 86 us -> 87.5 us (1.017)
  Pallas kernels: 81.2 us -> 82.7 us
    pallas_call x1, Pallas kernels: 81.2 us -> 82.7 us  [fused_local(): pl.pallas_call(fused, out_shape=jax.ShapeDtypeStruct((own, all_kc), jnp.f...]
where the time goes in v5:
time: 87.5 us; the launch traced here: 87.4 us
  Pallas kernels  82.7 us (95%)
  local copies, waits for them, and re-layouts  4.65 us (5%)
    pallas_call x1, Pallas kernels, fused_local(): pl.pallas_call(fused, out_shape=jax.ShapeDtypeStruct((own, all_kc), jnp.f...  82.7 us
    unnamed x1, local copies, waits for them, and re-layouts  4.65 us

profile of v5, /device:TPU:0, one launch (start us, length us, event | category | flops | bytes accessed | tf_op | source)
XLA Modules:
  0.0 87.4 jit_solution(14420807264892931030)
XLA Ops:
  0.0 82.7 %shard_map.28 = f32[256,4096]{1,0:T(8,128)} custom-call(bf16[128,1024]{1,0:T(8,128)(2,1)} %points_ref.1, bf16[4096,1024]{1,0:T(8,128)(2,1)} %cents_ref.1), custom_call_target="tpu_custom_call" | custom-call | flops 32212254720 | bytes 9437184 | tf_op jit(solution)/shard_map/pallas_call | solution.py:457
  82.7 4.7 %copy.4 = f32[256,4096]{1,0:T(8,128)} copy(f32[256,4096]{1,0:T(8,128)} %shard_map.28) | data formatting | bytes 8388608

commit v6 on v2

--- a/solution.py
+++ b/solution.py
@@ -65,6 +65,22 @@
 CHUNK = 1024
 
 
+ORDER = (
+    "c0", "x0", "y0", "c1", "x1", "c2", "y1", "d0",
+    "x2", "c3", "y2", "x3", "d1", "y3", "d2", "d3",
+)
+DIGITS = tuple(
+    tuple(
+        sum(f(b) << (2 * i) for i, b in enumerate(ORDER[h:h + 8])) for h in (0, 8)
+    )
+    for f in (lambda b: int(b[1]), lambda b: int(b[0] in "xd"), lambda b: int(b[0] in "yd"))
+)
+
+
+def order_digit(k, n):
+    return (jnp.where(n < 8, DIGITS[k][0], DIGITS[k][1]) >> (2 * (n % 8))) % 4
+
+
 def fused(
     points_ref, cents_ref, out_ref,
     x_ref, c_ref, e_ref, xt_ref, a_ref, bias_ref, buf0, buf1, obuf, mstat, scale_ref, gath,
@@ -236,26 +252,21 @@
         pzj, ppid, ptops, psums = carry
         for at, items in (
             (1, ((0, "x"), (0, "y"), (1, "c"))),
-            (2 + 4 * end, ((2, "c"),)),
-            (4, ((0, "d"), (1, "x"), (1, "y"))),
-            (5 + 5 * end, ((3, "c"),)),
-            (8, ((1, "d"), (2, "x"), (2, "y"))),
-            (12, ((2, "d"), (3, "x"), (3, "y"))),
-            (15, ((3, "d"),)),
+            (1 + 2 * end, ((2, "c"),)),
+            (3, ((1, "x"),)),
+            (3 + 2 * end, ((3, "c"),)),
+            (5, ((1, "y"), (0, "d"), (2, "x"))),
+            (7, ((2, "y"),)),
+            (9, ((3, "x"), (1, "d"))),
+            (11, ((3, "y"), (2, "d"))),
+            (14, ((3, "d"),)),
         ):
             @pl.when(n == at)
             def _(items=items):
                 for j, pos in items:
                     pass_on(j, pos)
 
-        g, r = n // 4, n % 4
-        last = n // 15
-        first = 1 - jnp.minimum(n, 1)
-        r0 = 1 - jnp.minimum(r, 1)
-        r3 = r // 3
-        j = g - r0 + first + r3 - last
-        fx = jnp.where(r == 1, 1, 0) + r0 - first + last
-        fy = jnp.where(r == 2, 1, 0) + r0 - first + last
+        j, fx, fy = (order_digit(k, n) for k in range(3))
         j1 = jnp.where(j == 1, 1, 0)
         j0 = jnp.where(j == 0, 1, 0)
         s = j0 * zz + j1 * (1 - zz) + (1 - j0 - j1) * j
@@ -283,7 +294,7 @@
             m, where = row_max(t8), rows
             tops.append(m)
 
-        for at, jj in ((5, 0), (9, 1), (13, 2)):
+        for at, jj in ((8, 0), (13, 1), (15, 2)):
             @pl.when(n == at)
             def _(jj=jj):
                 send_stats(jj)
@@ -319,37 +330,47 @@
 
     sub = obuf.shape[2]
     n_sub = CHUNK // sub
-
-    def out_copy(c, u):
-        col = pl.multiple_of(c * CHUNK + u * sub, sub)
-        return pltpu.make_async_copy(obuf.at[u], out_ref.at[:, pl.ds(col, sub)], out_sem.at[u])
-
-    def sums_step(c, _):
-        sc = scale_ref[pl.ds(c, 1), :]
-        a_ref[0:own_feats, :] = (xt_ref[...].astype(jnp.float32) * sc).astype(jnp.bfloat16)
+    slots = obuf.shape[0]
+    writes = []
+
+    def prepare(c):
+        sc = scale_ref[c:c + 1, :]
+        a = a_ref
+        a[0:own_feats, :] = (xt_ref[...].astype(jnp.float32) * sc).astype(jnp.bfloat16)
         hi = sc.astype(jnp.bfloat16).astype(jnp.float32)
-        lo = sc - hi
         which = lax.broadcasted_iota(jnp.int32, (16, sc.shape[1]), 0)
-        extra = jnp.where(which == 0, hi, jnp.where(which == 1, lo, 0.0))
-        a_ref[own_feats:own_feats + 16, :] = extra.astype(jnp.bfloat16)
+        extra = jnp.where(which == 0, hi, jnp.where(which == 1, sc - hi, 0.0))
+        a[own_feats:own_feats + 16, :] = extra.astype(jnp.bfloat16)
+
+    def multiply(c, u):
+        ks = slice(c * CHUNK + u * sub, c * CHUNK + (u + 1) * sub)
+        return lax.dot_general(
+            a_ref[...], e_ref[ks, :], NT, preferred_element_type=jnp.float32
+        )
+
+    def conclude(c, u, res):
+        ks = slice(c * CHUNK + u * sub, c * CHUNK + (u + 1) * sub)
+        counts = res[own_feats:own_feats + 1] + res[own_feats + 1:own_feats + 2]
+        own = c_ref[ks, own_col].astype(jnp.float32).T
+        t = len(writes)
+        if t >= slots:
+            writes[t - slots].wait()
+        obuf[t % slots] = (res[:own_feats] + PRIOR * own) * (1.0 / (counts + PRIOR))
+        copy = pltpu.make_async_copy(obuf.at[t % slots], out_ref.at[:, ks], out_sem.at[t % slots])
+        copy.start()
+        writes.append(copy)
+
+    pending = None
+    for c in range(n_chunk):
+        prepare(c)
         for u in range(n_sub):
-            ks = pl.ds(pl.multiple_of(c * CHUNK + u * sub, sub), sub)
-            res = lax.dot_general(a_ref[...], e_ref[ks, :], NT, preferred_element_type=jnp.float32)
-            counts = res[own_feats:own_feats + 1] + res[own_feats + 1:own_feats + 2]
-            inv = 1.0 / (counts + PRIOR)
-            own = c_ref[ks, own_col].astype(jnp.float32).T
-
-            @pl.when(c > 0)
-            def _(u=u):
-                out_copy(c - 1, u).wait()
-
-            obuf[u] = (res[:own_feats] + PRIOR * own) * inv
-            out_copy(c, u).start()
-        return 0
-
-    lax.fori_loop(0, n_chunk, sums_step, 0)
-    for u in range(n_sub):
-        out_copy(n_chunk - 1, u).wait()
+            res = multiply(c, u)
+            if pending is not None:
+                conclude(*pending)
+            pending = (c, u, res)
+    conclude(*pending)
+    for copy in writes[-slots:]:
+        copy.wait()
     for j in range(NZ):
         for pos in POS:
             each_route(j, pos, lambda c: c.wait_send())

time: 88.3 us -> 84.2 us (0.954)
  Pallas kernels: 83.5 us -> 79.4 us
    pallas_call x1, Pallas kernels: 83.5 us -> 79.4 us  [fused_local(): pl.pallas_call(fused, out_shape=jax.ShapeDtypeStruct((own, kc), jnp.float...]
where the time goes in v6:
time: 84.2 us; the launch traced here: 84 us
  Pallas kernels  79.4 us (94%)
  local copies, waits for them, and re-layouts  4.65 us (6%)
    pallas_call x1, Pallas kernels, fused_local(): pl.pallas_call(fused, out_shape=jax.ShapeDtypeStruct((own, kc), jnp.float...  79.4 us
    unnamed x1, local copies, waits for them, and re-layouts  4.65 us

profile of v6, /device:TPU:0, one launch (start us, length us, event | category | flops | bytes accessed | tf_op | source)
XLA Modules:
  0.0 84.0 jit_solution(4075837330719750674)
XLA Ops:
  0.0 79.4 %shard_map.28 = f32[256,4096]{1,0:T(8,128)} custom-call(bf16[128,1024]{1,0:T(8,128)(2,1)} %points_ref.1, bf16[4096,1024]{1,0:T(8,128)(2,1)} %cents_ref.1), custom_call_target="tpu_custom_call" | custom-call | flops 42949672960 | bytes 12582912 | tf_op jit(solution)/shard_map/pallas_call | solution.py:387
  79.4 4.7 %copy.4 = f32[256,4096]{1,0:T(8,128)} copy(f32[256,4096]{1,0:T(8,128)} %shard_map.28) | data formatting | bytes 8388608
